TPU v7x, 32 devices: a whole 2x2x4 slice. The times are simulated.
32 devices in a mesh: groups: 2 (over y), chol: 4 (over z), walk: 2 (over x), spin: 2 (over core).
Axes of the slice: x: 2, y: 2, z: 4, core: 2. Of those that a mesh axis runs over, the one named last changes fastest.
Arguments:
- orbitals: float32 [16, 2, 1400, 150], P(('groups', 'chol', 'walk'), 'spin'), parts along dimension 0, may hold values from -6 to 6
- intersection_inv: float32 [16, 2, 150, 150], P(('groups', 'chol', 'walk'), 'spin'), parts along dimension 0, may hold values from -0.5 to 0.5
- half_chol: bfloat16 [12, 2, 150, 1400], P('chol', 'spin'), may hold values from -0.013671875 to 0.013671875
- slab_chol: bfloat16 [12, 256, 1400], P('chol'), may hold values from -0.15625 to 0.15625
- aux_field: int32 [16, 12], P('groups', 'chol'), parts along dimension 0, may hold values from 0 to 2
Outputs:
- new_slab: float32 [16, 2, 256, 150], P(('groups', 'chol', 'walk'), 'spin'), parts along dimension 0
There are 2 independent parts, one for each index of `groups`. A program takes and returns all parts, laid end to end along the dimension named above; an argument that names none is the same for every part. Nothing has to cross between parts.
All inputs are finite; a program needn't handle non-finite values.
Results may differ from a plain program's by a relative error of at most 0.003.
Values may be sent and summed in bfloat16 or wider, within the bound.
A program may use at most 64 MiB of HBM per device.

v0:
```python
import math

import jax
import jax.numpy as jnp
from jax import lax
from jax.sharding import PartitionSpec as P

root_three = math.sqrt(3.0)


def body(orbitals, intersection_inv, half_chol, slab_chol, aux_field):
    cycle_size = lax.axis_size("chol")
    walk_index = lax.axis_index("walk")
    walkers_here = orbitals.shape[0]
    vectors_here = slab_chol.shape[0]
    slab_rows = slab_chol.shape[1]
    visitors = cycle_size * walkers_here
    orbital_piece = lax.all_gather(orbitals, "chol", axis=0, tiled=True)
    inverse_piece = lax.all_gather(intersection_inv, "chol", axis=0, tiled=True)
    rotated = jnp.einsum(
        "wsmk,wskn->wsmn", orbital_piece, inverse_piece, precision=lax.Precision.HIGHEST
    ).astype(jnp.bfloat16)
    lowered = orbital_piece[:, 0].astype(jnp.bfloat16)
    partial_value = jnp.einsum(
        "gsnm,wsmn->wg", half_chol, rotated, preferred_element_type=jnp.float32
    )
    item = jnp.einsum("grm,wmn->wgrn", slab_chol, lowered, preferred_element_type=jnp.float32)
    force_bias = lax.psum(partial_value, "spin")
    field_table = aux_field.reshape(cycle_size, aux_field.shape[0] // cycle_size, vectors_here)
    own_fields = lax.dynamic_slice_in_dim(field_table, walk_index * walkers_here, walkers_here, 1)
    own_fields = own_fields.reshape(visitors, vectors_here)
    shifts = root_three * (own_fields.astype(jnp.float32) - 1.0) - force_bias
    update = lax.psum_scatter(
        jnp.einsum("wg,wgrn->wrn", shifts, item, precision=lax.Precision.HIGHEST),
        "chol",
        scatter_dimension=0,
        tiled=True,
    )
    total_vectors = vectors_here * cycle_size
    updated = orbitals[:, :, :slab_rows, :] - update[:, None] / math.sqrt(total_vectors)
    return updated


def solution(mesh):
    placed = (
        P(("groups", "chol", "walk"), "spin", None, None),
        P(("groups", "chol", "walk"), "spin", None, None),
        P("chol", "spin", None, None),
        P("chol", None, None),
        P("groups", "chol"),
    )
    return jax.shard_map(
        body,
        mesh=mesh,
        in_specs=placed,
        out_specs=P(("groups", "chol", "walk"), "spin", None, None),
        check_vma=False,
    )
```

profile of v0, /device:TPU:0, one launch (start us, length us, event | category | flops | bytes accessed | tf_op | source)
XLA Modules:
  0.0 126.6 jit_solution(2216253055233050701)
XLA Ops:
  6.5 0.0 copy-start
  6.5 0.0 all-gather.2.cloned.1.call-start
  6.5 0.7 all-gather.2.cloned.1.call-update
  7.3 0.0 reduce-scatter.2.cloned.1.call-start
  7.3 0.8 copy.11
  8.1 22.0 %all_gather.7 = f32[4,1,150,150]{3,1,2,0:T(1,128)S(1)} all-gather(f32[1,1,150,150]{3,1,2,0:T(1,128)} %param.6), channel_id=1, replica_groups=mesh['groups'=2,'chol'=4,'walk'=2,'spin'=2] {'chol'}, dimensions={0}, use_global_device_ids=true | all-gather | bytes 450000 | tf_op jit(solution)/shard_map/all_gather | solution.py:19
  30.0 51.1 %all-gather.2.cloned.1.call-done = f32[4,1,1400,150]{2,1,3,0:T(1,128)} async-done(((f32[1,1,1400,150]{2,1,3,0:T(1,128)}), f32[4,1,1400,150]{2,1,3,0:T(1,128)}) %all-gather.2.cloned.1.call-update) | async-done | bytes 3360016 | tf_op jit(solution)/shard_map/all_gather | solution.py:18
  81.1 0.0 copy-start.1
  81.1 5.8 %fusion.3 = bf16[4,1400,150]{1,2,0:T(8,128)(2,1)S(1)} fusion(f32[4,1,1400,150]{2,1,3,0:T(1,128)} %all-gather.2.cloned.1.call-done, f32[4,1,150,150]{3,1,2,0:T(1,128)S(1)} %all_gather.7), kind=kOutput, calls=%fused_computation.4 | convolution fusion | flops 1512839936 | bytes 5400000 | tf_op jit(solution)/shard_map/wsmk,wskn->wsmn/dot_general | solution.py:20
  86.9 0.0 copy-done.1
  86.9 2.3 %fusion.14 = f32[4,3]{0,1:T(4,128)S(1)} fusion(bf16[3,150,1400]{2,1,0:T(8,128)(2,1)S(1)} %bitcast.40, bf16[4,1400,150]{1,2,0:T(8,128)(2,1)S(1)} %fusion.3), kind=kOutput, calls=%fused_computation.13 | convolution fusion | flops 5040000 | bytes 2940048 | tf_op jit(solution)/shard_map/gsnm,wsmn->wg/dot_general | solution.py:24
  89.2 0.1 copy.15
  89.3 2.5 %psum.7 = f32[4,3]{0,1:T(4,128)S(1)} all-reduce(f32[4,3]{0,1:T(4,128)S(1)} %fusion.14), channel_id=1, replica_groups=mesh['groups'=2,'chol'=4,'walk'=2,'spin'=2] {'spin'}, use_global_device_ids=true, to_apply=%region_0.0 | all-reduce | flops 12 | bytes 96 | tf_op jit(solution)/shard_map/psum | solution.py:28
  91.8 0.1 copy.27
  91.9 0.0 copy-done
  91.9 4.4 %fusion.8 = f32[4,256,150]{1,2,0:T(8,128)} fusion(bf16[3,256,1400]{1,2,0:T(8,128)(2,1)S(1)} %copy-done, f32[4,1,1400,150]{2,1,3,0:T(1,128)} %all-gather.2.cloned.1.call-done, f32[4,3]{1,0:T(4,128)S(1)} %copy.27), kind=kOutput, calls=%fused_computation.8 | convolution fusion | flops 1291008000 | bytes 6124848 | tf_op jit(solution)/shard_map/grm,wmn->wgrn/dot_general | solution.py:27
  96.3 0.0 reduce-scatter.2.cloned.1.call-update
  96.3 1.0 slice.3
  97.4 20.6 %reduce-scatter.2.cloned.1.call-done = f32[1,256,150]{1,2,0:T(8,128)} async-done(((f32[4,256,150]{1,2,0:T(8,128)}), f32[1,256,150]{1,2,0:T(8,128)}) %reduce-scatter.2.cloned.1.call-update) | async-done | bytes 153616 | tf_op jit(solution)/shard_map/reduce_scatter | solution.py:33
  118.0 0.9 copy_subtract_fusion
  118.9 0.8 copy.16
  (2 shorter events, 0.0 us)
Async XLA Ops:
  6.5 85.3 %copy-start = (bf16[3,256,1400]{1,2,0:T(8,128)(2,1)S(1)}, bf16[3,256,1400]{1,2,0:T(8,128)(2,1)}, u32[]{:S(2)}) copy-start(bf16[3,256,1400]{1,2,0:T(8,128)(2,1)} %param.8) | copy-start | bytes 6451204
  6.5 74.6 %all-gather.2.cloned.1.call-start = ((), (), s32[]{:S(2)}) async-start(), calls=%async_computation.1 | async-start | bytes 4224000 | tf_op jit(solution)/shard_map/all_gather | solution.py:18
  7.3 110.7 %reduce-scatter.2.cloned.1.call-start = ((), (), s32[]{:S(2)}) async-start(), calls=%async_computation.2 | async-start | bytes 778240 | tf_op jit(solution)/shard_map/reduce_scatter | solution.py:33
  81.1 5.8 %copy-start.1 = (bf16[3,1,150,1400]{3,2,1,0:T(8,128)(2,1)S(1)}, bf16[3,1,150,1400]{3,2,1,0:T(8,128)(2,1)}, u32[]{:S(2)}) copy-start(bf16[3,1,150,1400]{3,2,1,0:T(8,128)(2,1)} %param.7) | copy-start | bytes 3780004
Sparse Core Ops, SparseCore 0:
  8.9 72.1 all-gather.1
  96.5 21.4 reduce-scatter.1
where the time goes:
time: 127 us
  waiting for transfers between devices  72.4 us (57%)
  blocking collectives  24.4 us (19%)
  between operations  13.4 us (11%)
  matrix products  12.5 us (10%)
  local copies, waits for them, and re-layouts  2.79 us (2%)
    all_gather x1, waiting for transfers between devices, body(): orbital_piece = lax.all_gather(orbitals, 'chol', axis=0, tiled=True)  51.1 us
    all_gather x1, blocking collectives, body(): inverse_piece = lax.all_gather(intersection_inv, 'chol', axis=0, tiled=True)  22 us
    reduce_scatter x1, waiting for transfers between devices, body(): lax.psum_scatter(jnp.einsum('wg,wgrn->wrn', shifts, item, precision=lax.P...  20.6 us
    dot_general x1, matrix products, body(): jnp.einsum('wsmk,wskn->wsmn', orbital_piece, inverse_piece, precision=lax...  5.78 us
    dot_general x1, matrix products, body(): jnp.einsum('grm,wmn->wgrn', slab_chol, lowered, preferred_element_type=jn...  4.44 us
  transfers between devices with their start and end apart: 2, of which 2 were waited for; matrix products, arithmetic and copies ran while one was open for 1% of the time, Pallas kernels for 0%

commit v1 on v0

v1 whole, which is shorter than its diff:
```python
import functools
import math

import jax
import jax.numpy as jnp
from jax import lax
from jax.experimental import pallas as pl
from jax.experimental.pallas import tpu as pltpu
from jax.sharding import PartitionSpec as P

MESH = pl.DeviceIdType.MESH
root_three = math.sqrt(3.0)
NT = (((1,), (1,)), ((), ()))


def up_to(value, step):
    return -(-value // step) * step


def kernel(line, walks, orb_hbm, inv_hbm, half_hbm, slab_hbm, aux_ref, out_ref,
           orb, inv, half, slab, buf, invb, item, fbv, fbo, upd, acc, own, load_sem,
           walk_send, walk_recv, inv_send, inv_recv, fb_send, fb_recv, upd_send, upd_recv):
    me = lax.axis_index("chol")
    spin = lax.axis_index("spin")
    wx = lax.axis_index("walk")
    basis, elec = orb.shape
    vectors = half.shape[0]
    rows = slab.shape[1]
    tall = buf.shape[1]
    scale = 1.0 / math.sqrt(vectors * line)

    loads = [pltpu.make_async_copy(src, dst, load_sem.at[i]) for i, (src, dst) in enumerate(
        ((orb_hbm, orb), (inv_hbm, inv), (half_hbm, half), (slab_hbm, slab)))]
    for load in loads:
        load.start()

    barrier = pltpu.get_barrier_semaphore()
    for k in range(1, line):
        pl.semaphore_signal(barrier, inc=1, device_id={"chol": lax.rem(me + k, line)}, device_id_type=MESH)
    pl.semaphore_signal(barrier, inc=1, device_id={"spin": 1 - spin}, device_id_type=MESH)

    loads[0].wait()
    loads[1].wait()
    eye = (lax.broadcasted_iota(jnp.int32, (tall, elec), 0)
           == lax.broadcasted_iota(jnp.int32, (tall, elec), 1)).astype(jnp.bfloat16)
    invb[me] = jnp.dot(eye, inv[...].astype(jnp.bfloat16), preferred_element_type=jnp.float32).astype(jnp.bfloat16)
    wide = buf.shape[2]
    for start in range(0, basis, 256):
        size = min(256, basis - start)
        piece = lax.dot_general(eye, orb[start:start + size, :].astype(jnp.bfloat16), NT,
                                preferred_element_type=jnp.float32).astype(jnp.bfloat16)
        end = min(start + 256, wide)
        if end - start > size:
            piece = jnp.concatenate([piece, jnp.zeros((tall, end - start - size), jnp.bfloat16)], axis=1)
        buf[me, :, start:end] = piece

    pl.semaphore_wait(barrier, line)

    def copies(q, way, to):
        return (
            pltpu.make_async_remote_copy(invb.at[q], invb.at[q], inv_send.at[way, q], inv_recv.at[q],
                                         device_id={"chol": to}, device_id_type=MESH),
            pltpu.make_async_remote_copy(buf.at[q], buf.at[q], walk_send.at[way, q], walk_recv.at[q],
                                         device_id={"chol": to}, device_id_type=MESH),
        )

    def send_up(q):
        @pl.when(me < line - 1)
        def _():
            for copy in copies(q, 0, me + 1):
                copy.start()

    def send_down(q):
        @pl.when(me > 0)
        def _():
            for copy in copies(q, 1, me - 1):
                copy.start()

    def arrive(q):
        for copy in copies(q, 0, lax.rem(me + 1, line)):
            copy.wait_recv()

    def bias_copy(q):
        return pltpu.make_async_remote_copy(fbv.at[q], fbo.at[q], fb_send.at[q], fb_recv.at[q],
                                            device_id={"spin": 1 - spin}, device_id_type=MESH)

    def update_copy(q):
        return pltpu.make_async_remote_copy(upd.at[q], acc.at[me], upd_send.at[q], upd_recv.at[me],
                                            device_id={"chol": q}, device_id_type=MESH)

    def compute(q, slot):
        x = buf[q, :, 0:basis]
        inverse = invb[q].astype(jnp.float32)
        for g in range(vectors):
            met = lax.dot_general(x, half[g], NT, preferred_element_type=jnp.float32)
            part = jnp.sum(jnp.sum(met * inverse, axis=0, keepdims=True), axis=1, keepdims=True)
            fbv[q, g:g + 1, :] = jnp.broadcast_to(part, (1, rows))
        bias_copy(q).start()
        for g in range(vectors):
            item[slot, g] = lax.dot_general(x, slab[g], NT, preferred_element_type=jnp.float32)

    def updated(q, slot):
        bias_copy(q).wait_recv()
        bias = fbv[q] + fbo[q]
        total = None
        for g in range(vectors):
            field = aux_ref[q * walks + wx, g]
            shift = root_three * (field.astype(jnp.float32) - 1.0) - bias[g:g + 1, :]
            term = item[slot, g] * (shift * scale)
            total = term if total is None else total + term
        return total

    send_up(me)
    send_down(me)
    loads[2].wait()
    loads[3].wait()
    fbv[...] = jnp.zeros_like(fbv)
    compute(me, 0)
    own[...] = updated(me, 0)

    def level(d, carry):
        above, below = me + d, me - d

        @pl.when(above < line)
        def _():
            arrive(above)
            send_down(above)

        @pl.when(below >= 0)
        def _():
            arrive(below)
            send_up(below)

        def meet(side, carry):
            q = me + d - 2 * d * side

            @pl.when((q >= 0) & (q < line))
            def _():
                compute(q, side)
            return carry

        def give(side, carry):
            q = me + d - 2 * d * side

            @pl.when((q >= 0) & (q < line))
            def _():
                upd[q] = updated(q, side).astype(jnp.bfloat16)
                update_copy(q).start()
            return carry

        lax.fori_loop(0, 2, meet, 0)
        lax.fori_loop(0, 2, give, 0)
        return carry

    lax.fori_loop(1, line, level, 0)

    total = own[...]
    for k in range(1, line):
        q = lax.rem(me + k, line)
        pltpu.make_async_remote_copy(upd.at[q], acc.at[q], upd_send.at[q], upd_recv.at[q],
                                     device_id={"chol": q}, device_id_type=MESH).wait_recv()
        total = total + acc[q].astype(jnp.float32)
    out_ref[...] = orb[0:rows, :] - jnp.transpose(total)[:, 0:elec]

    def drain(q, carry):
        @pl.when((q <= me) & (me < line - 1))
        def _():
            for copy in copies(q, 0, lax.rem(me + 1, line)):
                copy.wait_send()

        @pl.when((q >= me) & (me > 0))
        def _():
            for copy in copies(q, 1, lax.rem(me + line - 1, line)):
                copy.wait_send()

        bias_copy(q).wait_send()

        @pl.when(q != me)
        def _():
            update_copy(q).wait_send()
        return carry

    lax.fori_loop(0, line, drain, 0)


def body(orbitals, intersection_inv, half_chol, slab_chol, aux_field):
    line = lax.axis_size("chol")
    walks = lax.axis_size("walk")
    basis, elec = orbitals.shape[2:]
    vectors, rows = slab_chol.shape[:2]
    tall, wide = up_to(elec, 32), up_to(basis, 128)
    bf16, f32 = jnp.bfloat16, jnp.float32
    dma = pltpu.SemaphoreType.DMA
    any_spec = pl.BlockSpec(memory_space=pl.ANY)
    out = pl.pallas_call(
        functools.partial(kernel, line, walks),
        out_shape=jax.ShapeDtypeStruct((rows, elec), f32),
        in_specs=[any_spec] * 4 + [pl.BlockSpec(memory_space=pltpu.SMEM)],
        out_specs=pl.BlockSpec(memory_space=pltpu.VMEM),
        scratch_shapes=[
            pltpu.VMEM((basis, elec), f32),
            pltpu.VMEM((elec, elec), f32),
            pltpu.VMEM((vectors, elec, basis), bf16),
            pltpu.VMEM((vectors, rows, basis), bf16),
            pltpu.VMEM((line, tall, wide), bf16),
            pltpu.VMEM((line, tall, elec), bf16),
            pltpu.VMEM((2, vectors, tall, rows), f32),
            pltpu.VMEM((line, up_to(vectors, 8), rows), f32),
            pltpu.VMEM((line, up_to(vectors, 8), rows), f32),
            pltpu.VMEM((line, tall, rows), bf16),
            pltpu.VMEM((line, tall, rows), bf16),
            pltpu.VMEM((tall, rows), f32),
            dma((4,)),
            dma((2, line)), dma((line,)),
            dma((2, line)), dma((line,)),
            dma((line,)), dma((line,)),
            dma((line,)), dma((line,)),
        ],
        compiler_params=pltpu.CompilerParams(
            collective_id=0, has_side_effects=True, vmem_limit_bytes=48 * 1024 * 1024
        ),
    )(orbitals[0, 0], intersection_inv[0, 0], half_chol[:, 0], slab_chol, aux_field)
    return out[None, None]


def solution(mesh):
    placed = (
        P(("groups", "chol", "walk"), "spin", None, None),
        P(("groups", "chol", "walk"), "spin", None, None),
        P("chol", "spin", None, None),
        P("chol", None, None),
        P("groups", "chol"),
    )
    return jax.shard_map(
        body,
        mesh=mesh,
        in_specs=placed,
        out_specs=P(("groups", "chol", "walk"), "spin", None, None),
        check_vma=False,
    )
```

time: 127 us -> 67.1 us (0.53)
  waiting for transfers between devices: 72.4 us -> 0 us
  Pallas kernels: 0 us -> 53.4 us
  blocking collectives: 24.4 us -> 0 us
  between operations: 13.4 us -> 0.04 us
  matrix products: 12.5 us -> 0 us
  local copies, waits for them, and re-layouts: 2.79 us -> 13.4 us
    pallas_call x0 -> x1, Pallas kernels: none -> 53.4 us  [body(): pl.pallas_call(functools.partial(kernel, line, walks), out_shape=jax.Shap...]
    all_gather x1 -> x0, waiting for transfers between devices: 51.1 us -> none  [body(): orbital_piece = lax.all_gather(orbitals, 'chol', axis=0, tiled=True)]
    all_gather x1 -> x0, blocking collectives: 22 us -> none  [body(): inverse_piece = lax.all_gather(intersection_inv, 'chol', axis=0, tiled=True)]
    reduce_scatter x1 -> x0, waiting for transfers between devices: 20.6 us -> none  [body(): lax.psum_scatter(jnp.einsum('wg,wgrn->wrn', shifts, item, precision=lax.P...]
    dot_general x3 -> x0, matrix products: 12.5 us -> none  [the longest x1 5.78 us: body(): jnp.einsum('wsmk,wskn->wsmn', orbital_piece, inverse_piece, precision=lax...]
    unnamed x6 -> x12, local copies, waits for them, and re-layouts: 0.86 us -> 11.6 us
    psum x1 -> x0, blocking collectives: 2.46 us -> none  [body(): force_bias = lax.psum(partial_value, 'spin')]
    broadcast_in_dim x0 -> x1, local copies, waits for them, and re-layouts: none -> 1.73 us  [body(): return out[None, None]]
  transfers between devices with their start and end apart: 2 -> 0, of which waited for: 2 -> 0; matrix products, arithmetic and copies ran while one was open for 1% -> 0% of each run, Pallas kernels for 0% -> 0%
where the time goes in v1:
time: 67.1 us; the launch traced here: 66.8 us
  Pallas kernels  53.4 us (80%)
  local copies, waits for them, and re-layouts  13.4 us (20%)
    pallas_call x1, Pallas kernels, body(): pl.pallas_call(functools.partial(kernel, line, walks), out_shape=jax.Shap...  53.4 us
    unnamed x12, local copies, waits for them, and re-layouts  11.6 us
    broadcast_in_dim x1, local copies, waits for them, and re-layouts, body(): return out[None, None]  1.73 us

profile of v1, /device:TPU:0, one launch (start us, length us, event | category | flops | bytes accessed | tf_op | source)
XLA Modules:
  0.0 66.8 jit_solution(7877807256516120894)
XLA Ops:
  0.0 0.8 %copy.8.aux_ref = s32[8,3]{1,0:T(8,128)S(1)} copy(s32[8,3]{0,1:T(4,128)} %param.9) | data formatting | bytes 192 | tf_op args[4]
  0.8 1.6 %copy.12 = f32[1,1,150,150]{3,2,1,0:T(8,128)} copy(f32[1,1,150,150]{3,1,2,0:T(1,128)} %param.6) | data formatting | bytes 180000
  2.3 3.3 %copy.6 = f32[1,1,1400,150]{3,2,1,0:T(8,128)} copy(f32[1,1,1400,150]{2,1,3,0:T(1,128)} %param.5) | data formatting | bytes 1680000 | tf_op args[0]
  5.6 0.0 copy-start.1
  5.6 3.0 %copy.7.slab_hbm = bf16[3,256,1400]{2,1,0:T(8,128)(2,1)S(1)} copy(bf16[3,256,1400]{1,2,0:T(8,128)(2,1)} %param.8) | data formatting | bytes 4300800 | tf_op args[3]
  8.7 0.0 copy-done.1
  8.7 0.0 copy-start
  8.7 1.4 %copy-done = f32[1,1,1400,150]{3,2,1,0:T(8,128)S(1)} copy-done((f32[1,1,1400,150]{3,2,1,0:T(8,128)S(1)}, f32[1,1,1400,150]{3,2,1,0:T(8,128)}, u32[]{:S(2)}) %copy-start) | copy-done | bytes 840024
  10.1 0.0 copy-start.3
  10.1 0.9 %copy-done.3 = f32[1,1,150,150]{3,2,1,0:T(8,128)S(1)} copy-done((f32[1,1,150,150]{3,2,1,0:T(8,128)S(1)}, f32[1,1,150,150]{3,2,1,0:T(8,128)}, u32[]{:S(2)}) %copy-start.3) | copy-done | bytes 90024
  11.0 53.4 %shard_map.55 = f32[256,150]{1,0:T(8,128)S(1)} custom-call(f32[1400,150]{1,0:T(8,128)S(1)} %bitcast.6, f32[150,150]{1,0:T(8,128)S(1)} %bitcast.9, bf16[3,150,1400]{2,1,0:T(8,128)(2,1)S(1)} %bitcast.7, bf16[3,256,1400]{2,1,0:T(8,128)(2,1)S(1)} %copy.7.slab_hbm, s32[8,3]{1,0:T(8,128)S(1)} %copy.8.aux_ref), custom_call_target="tpu_custom_call" | custom-call | tf_op jit(solution)/shard_map/pallas_call | solution.py:195
  64.4 0.0 copy-start.2
  64.4 0.7 %copy-done.2 = f32[256,150]{1,0:T(8,128)} copy-done((f32[256,150]{1,0:T(8,128)}, f32[256,150]{1,0:T(8,128)S(1)}, u32[]{:S(2)}) %copy-start.2) | copy-done | bytes 153624
  65.1 1.7 %copy.9 = f32[1,1,256,150]{2,1,3,0:T(1,128)} copy(f32[1,1,256,150]{3,2,1,0:T(8,128)} %bitcast.8) | data formatting | bytes 307200 | tf_op jit(solution)/shard_map/broadcast_in_dim | solution.py:223
Async XLA Ops:
  5.6 3.1 %copy-start.1 = (bf16[3,1,150,1400]{3,2,1,0:T(8,128)(2,1)S(1)}, bf16[3,1,150,1400]{3,2,1,0:T(8,128)(2,1)}, u32[]{:S(2)}) copy-start(bf16[3,1,150,1400]{3,2,1,0:T(8,128)(2,1)} %param.7) | copy-start | bytes 3780004
  8.7 1.4 %copy-start = (f32[1,1,1400,150]{3,2,1,0:T(8,128)S(1)}, f32[1,1,1400,150]{3,2,1,0:T(8,128)}, u32[]{:S(2)}) copy-start(f32[1,1,1400,150]{3,2,1,0:T(8,128)} %copy.6) | copy-start | bytes 2520004
  10.1 0.9 %copy-start.3 = (f32[1,1,150,150]{3,2,1,0:T(8,128)S(1)}, f32[1,1,150,150]{3,2,1,0:T(8,128)}, u32[]{:S(2)}) copy-start(f32[1,1,150,150]{3,2,1,0:T(8,128)} %copy.12) | copy-start | bytes 270004
  64.4 0.7 %copy-start.2 = (f32[256,150]{1,0:T(8,128)}, f32[256,150]{1,0:T(8,128)S(1)}, u32[]{:S(2)}) copy-start(f32[256,150]{1,0:T(8,128)S(1)} %shard_map.55) | copy-start | bytes 460804

commit v2 on v1

--- a/solution.py
+++ b/solution.py
@@ -17,20 +17,22 @@
     return -(-value // step) * step
 
 
-def kernel(line, walks, orb_hbm, inv_hbm, half_hbm, slab_hbm, aux_ref, out_ref,
-           orb, inv, half, slab, buf, invb, item, fbv, fbo, upd, acc, own, load_sem,
+def kernel(line, walks, orb_hbm, inv_hbm, half_hbm, slab_hbm, aux_ref, out_hbm,
+           orb, inv, half, slab, res, buf, invb, item, fbv, fbo, upd, acc, own, load_sem,
            walk_send, walk_recv, inv_send, inv_recv, fb_send, fb_recv, upd_send, upd_recv):
     me = lax.axis_index("chol")
     spin = lax.axis_index("spin")
     wx = lax.axis_index("walk")
-    basis, elec = orb.shape
+    elec, basis = orb.shape
     vectors = half.shape[0]
-    rows = slab.shape[1]
+    rows = slab.shape[2]
+    lanes = invb.shape[2]
+    rest = elec - lanes
     tall = buf.shape[1]
     scale = 1.0 / math.sqrt(vectors * line)
 
     loads = [pltpu.make_async_copy(src, dst, load_sem.at[i]) for i, (src, dst) in enumerate(
-        ((orb_hbm, orb), (inv_hbm, inv), (half_hbm, half), (slab_hbm, slab)))]
+        ((orb_hbm.at[:, 0, :], orb), (inv_hbm.at[:, 0, :], inv), (half_hbm, half), (slab_hbm, slab)))]
     for load in loads:
         load.start()
 
@@ -43,16 +45,19 @@
     loads[1].wait()
     eye = (lax.broadcasted_iota(jnp.int32, (tall, elec), 0)
            == lax.broadcasted_iota(jnp.int32, (tall, elec), 1)).astype(jnp.bfloat16)
-    invb[me] = jnp.dot(eye, inv[...].astype(jnp.bfloat16), preferred_element_type=jnp.float32).astype(jnp.bfloat16)
+    tall_inv = jnp.dot(eye, inv[...].astype(jnp.bfloat16), preferred_element_type=jnp.float32)
+    invb[me, 0:tall, :] = tall_inv[:, 0:lanes].astype(jnp.bfloat16)
+    side = [tall_inv[at:at + 32, lanes:elec] for at in range(0, tall, 32)]
+    side.append(jnp.zeros((32, lanes - rest * len(side)), jnp.float32))
+    invb[me, tall:tall + 32, :] = jnp.concatenate(side, axis=1).astype(jnp.bfloat16)
     wide = buf.shape[2]
-    for start in range(0, basis, 256):
-        size = min(256, basis - start)
-        piece = lax.dot_general(eye, orb[start:start + size, :].astype(jnp.bfloat16), NT,
-                                preferred_element_type=jnp.float32).astype(jnp.bfloat16)
-        end = min(start + 256, wide)
-        if end - start > size:
-            piece = jnp.concatenate([piece, jnp.zeros((tall, end - start - size), jnp.bfloat16)], axis=1)
-        buf[me, :, start:end] = piece
+    full = elec // 16 * 16
+    last = basis // 128 * 128
+    buf[me, :, last:wide] = jnp.zeros((tall, wide - last), jnp.bfloat16)
+    buf[me, 0:full, 0:basis] = orb[0:full, :].astype(jnp.bfloat16)
+    buf[me, full:tall, 0:basis] = jnp.dot(
+        eye[0:tall - full, 0:elec - full], orb[full:elec, :].astype(jnp.bfloat16),
+        preferred_element_type=jnp.float32).astype(jnp.bfloat16)
 
     pl.semaphore_wait(barrier, line)
 
@@ -90,21 +95,25 @@
 
     def compute(q, slot):
         x = buf[q, :, 0:basis]
-        inverse = invb[q].astype(jnp.float32)
+        packed = invb[q].astype(jnp.float32)
         for g in range(vectors):
             met = lax.dot_general(x, half[g], NT, preferred_element_type=jnp.float32)
-            part = jnp.sum(jnp.sum(met * inverse, axis=0, keepdims=True), axis=1, keepdims=True)
+            part = jnp.sum(met[:, 0:lanes] * packed[0:tall, :], axis=0, keepdims=True)
+            part = jnp.sum(part, axis=1, keepdims=True)
+            for i in range(tall // 32):
+                beside = met[32 * i:32 * i + 32, lanes:elec] * packed[tall:, rest * i:rest * i + rest]
+                part = part + jnp.sum(jnp.sum(beside, axis=0, keepdims=True), axis=1, keepdims=True)
             fbv[q, g:g + 1, :] = jnp.broadcast_to(part, (1, rows))
         bias_copy(q).start()
         for g in range(vectors):
-            item[slot, g] = lax.dot_general(x, slab[g], NT, preferred_element_type=jnp.float32)
+            item[slot, g] = jnp.dot(x, slab[g], preferred_element_type=jnp.float32)
 
     def updated(q, slot):
         bias_copy(q).wait_recv()
         bias = fbv[q] + fbo[q]
         total = None
         for g in range(vectors):
-            field = aux_ref[q * walks + wx, g]
+            field = aux_ref[g, q * walks + wx]
             shift = root_three * (field.astype(jnp.float32) - 1.0) - bias[g:g + 1, :]
             term = item[slot, g] * (shift * scale)
             total = term if total is None else total + term
@@ -160,7 +169,10 @@
         pltpu.make_async_remote_copy(upd.at[q], acc.at[q], upd_send.at[q], upd_recv.at[q],
                                      device_id={"chol": q}, device_id_type=MESH).wait_recv()
         total = total + acc[q].astype(jnp.float32)
-    out_ref[...] = orb[0:rows, :] - jnp.transpose(total)[:, 0:elec]
+    res[...] = orb[:, 0:rows] - total[0:elec, :]
+    leave = pltpu.make_async_copy(res, out_hbm.at[:, 0, :], load_sem.at[0])
+    leave.start()
+    leave.wait()
 
     def drain(q, carry):
         @pl.when((q <= me) & (me < line - 1))
@@ -194,16 +206,17 @@
     any_spec = pl.BlockSpec(memory_space=pl.ANY)
     out = pl.pallas_call(
         functools.partial(kernel, line, walks),
-        out_shape=jax.ShapeDtypeStruct((rows, elec), f32),
+        out_shape=jax.ShapeDtypeStruct((elec, 1, rows), f32),
         in_specs=[any_spec] * 4 + [pl.BlockSpec(memory_space=pltpu.SMEM)],
-        out_specs=pl.BlockSpec(memory_space=pltpu.VMEM),
+        out_specs=any_spec,
         scratch_shapes=[
-            pltpu.VMEM((basis, elec), f32),
+            pltpu.VMEM((elec, basis), f32),
             pltpu.VMEM((elec, elec), f32),
             pltpu.VMEM((vectors, elec, basis), bf16),
-            pltpu.VMEM((vectors, rows, basis), bf16),
+            pltpu.VMEM((vectors, basis, rows), bf16),
+            pltpu.VMEM((elec, rows), f32),
             pltpu.VMEM((line, tall, wide), bf16),
-            pltpu.VMEM((line, tall, elec), bf16),
+            pltpu.VMEM((line, tall + 32, 128), bf16),
             pltpu.VMEM((2, vectors, tall, rows), f32),
             pltpu.VMEM((line, up_to(vectors, 8), rows), f32),
             pltpu.VMEM((line, up_to(vectors, 8), rows), f32),
@@ -217,10 +230,13 @@
             dma((line,)), dma((line,)),
         ],
         compiler_params=pltpu.CompilerParams(
-            collective_id=0, has_side_effects=True, vmem_limit_bytes=48 * 1024 * 1024
+            collective_id=0, has_side_effects=True, vmem_limit_bytes=63 * 1024 * 1024
         ),
-    )(orbitals[0, 0], intersection_inv[0, 0], half_chol[:, 0], slab_chol, aux_field)
-    return out[None, None]
+    )(
+        jnp.transpose(orbitals[0], (2, 0, 1)), jnp.transpose(intersection_inv[0], (1, 0, 2)),
+        half_chol[:, 0], jnp.transpose(slab_chol, (0, 2, 1)), jnp.transpose(aux_field),
+    )
+    return jnp.transpose(out, (1, 2, 0))[None]
 
 
 def solution(mesh):

time: 67.1 us -> 53.2 us (0.79)
  local copies, waits for them, and re-layouts: 13.4 us -> 1.68 us
  Pallas kernels: 53.4 us -> 51.4 us
    unnamed x12 -> x1, local copies, waits for them, and re-layouts: 11.6 us -> 1.68 us
    pallas_call x1, Pallas kernels: 53.4 us -> 51.4 us  [body(): pl.pallas_call(functools.partial(kernel, line, walks), out_shape=jax.Shap...]
    broadcast_in_dim x1 -> x0, local copies, waits for them, and re-layouts: 1.73 us -> none  [body(): return out[None, None]]
where the time goes in v2:
time: 53.2 us; the launch traced here: 53.1 us
  Pallas kernels  51.4 us (97%)
  local copies, waits for them, and re-layouts  1.68 us (3%)
    pallas_call x1, Pallas kernels, body(): pl.pallas_call(functools.partial(kernel, line, walks), out_shape=jax.Shap...  51.4 us
    unnamed x1, local copies, waits for them, and re-layouts  1.68 us

profile of v2, /device:TPU:0, one launch (start us, length us, event | category | flops | bytes accessed | tf_op | source)
XLA Modules:
  0.0 53.1 jit_solution(3405225385804922780)
XLA Ops:
  0.0 51.4 %shard_map.55 = f32[150,1,256]{2,1,0:T(1,128)} custom-call(f32[150,1,1400]{2,1,0:T(1,128)} %bitcast.14, f32[150,1,150]{2,1,0:T(1,128)} %bitcast.16, bf16[3,150,1400]{2,1,0:T(8,128)(2,1)} %bitcast.13, bf16[3,1400,256]{2,1,0:T(8,128)(2,1)} %bitcast.12, s32[3,8]{1,0:T(4,128)} %bitcast.17), custom_call_target="tpu_custom_call" | custom-call | tf_op jit(solution)/shard_map/pallas_call | solution.py:207
  51.4 1.7 %copy.8 = f32[1,1,256,150]{2,1,3,0:T(1,128)} copy(f32[1,1,256,150]{2,1,3,0:T(1,128)} %bitcast.15) | data formatting | bytes 307200

commit v3 on v2

v3 whole, which is shorter than its diff:
```python
import functools
import math

import jax
import jax.numpy as jnp
from jax import lax
from jax.experimental import pallas as pl
from jax.experimental.pallas import tpu as pltpu
from jax.sharding import PartitionSpec as P

MESH = pl.DeviceIdType.MESH
root_three = math.sqrt(3.0)
NT = (((1,), (1,)), ((), ()))


def up_to(value, step):
    return -(-value // step) * step


def kernel(line, walks, orb_hbm, inv_hbm, half_hbm, slab_hbm, aux_ref, out_hbm,
           orb, inv, half, slab, half_end, slab_end, res, buf, invb, item, fbv, fbo, fbe, upd, acc, total, load_sem,
           walk_send, walk_recv, inv_send, inv_recv, fb_send, fb_recv, mate_send, mate_recv, upd_send, upd_recv,
           end_send, end_recv):
    me = lax.axis_index("chol")
    spin = lax.axis_index("spin")
    wx = lax.axis_index("walk")
    elec, basis = orb.shape
    vectors = half.shape[0]
    rows = slab.shape[2]
    lanes = invb.shape[2]
    rest = elec - lanes
    tall, wide = buf.shape[1:]
    cut = basis - slab_end.shape[1]
    scale = 1.0 / math.sqrt(vectors * line)
    is_end = (me == 0) | (me == line - 1)
    is_helper = (me == 1) | (me == line - 2)
    mate = jnp.where(me == 0, 1, jnp.where(me == 1, 0, jnp.where(me == line - 1, line - 2, line - 1)))
    end = jnp.where(is_end, me, mate)

    loads = [pltpu.make_async_copy(src, dst, load_sem.at[i]) for i, (src, dst) in enumerate(
        ((orb_hbm.at[:, 0, :], orb), (inv_hbm.at[:, 0, :], inv), (half_hbm, half), (slab_hbm, slab)))]
    for load in loads:
        load.start()

    barrier = pltpu.get_barrier_semaphore()
    for k in range(1, line):
        pl.semaphore_signal(barrier, inc=1, device_id={"chol": lax.rem(me + k, line)}, device_id_type=MESH)
    pl.semaphore_signal(barrier, inc=1, device_id={"spin": 1 - spin}, device_id_type=MESH)


    @pl.when(is_end | is_helper)
    def _():
        pl.semaphore_signal(barrier, inc=1, device_id={"chol": mate, "spin": 1 - spin}, device_id_type=MESH)

    loads[0].wait()
    loads[1].wait()
    eye = (lax.broadcasted_iota(jnp.int32, (tall, elec), 0)
           == lax.broadcasted_iota(jnp.int32, (tall, elec), 1)).astype(jnp.bfloat16)
    tall_inv = jnp.dot(eye, inv[...].astype(jnp.bfloat16), preferred_element_type=jnp.float32)
    invb[me, 0:tall, :] = tall_inv[:, 0:lanes].astype(jnp.bfloat16)
    side = [tall_inv[at:at + 32, lanes:elec] for at in range(0, tall, 32)]
    side.append(jnp.zeros((32, lanes - rest * len(side)), jnp.float32))
    invb[me, tall:tall + 32, :] = jnp.concatenate(side, axis=1).astype(jnp.bfloat16)
    full = elec // 16 * 16
    last = basis // 128 * 128
    buf[me, :, last:wide] = jnp.zeros((tall, wide - last), jnp.bfloat16)
    buf[me, 0:full, 0:basis] = orb[0:full, :].astype(jnp.bfloat16)
    buf[me, full:tall, 0:basis] = jnp.dot(
        eye[0:tall - full, 0:elec - full], orb[full:elec, :].astype(jnp.bfloat16),
        preferred_element_type=jnp.float32).astype(jnp.bfloat16)

    pl.semaphore_wait(barrier, line + jnp.where(is_end | is_helper, 1, 0))

    def copies(q, way, to):
        where = {"chol": to}
        first, last = buf.at[q, :, 0:cut], buf.at[q, :, cut:wide]
        return (
            pltpu.make_async_remote_copy(invb.at[q], invb.at[q], inv_send.at[way, q], inv_recv.at[q],
                                         device_id=where, device_id_type=MESH),
            pltpu.make_async_remote_copy(first, first, walk_send.at[way, 0, q], walk_recv.at[0, q],
                                         device_id=where, device_id_type=MESH),
            pltpu.make_async_remote_copy(last, last, walk_send.at[way, 1, q], walk_recv.at[1, q],
                                         device_id=where, device_id_type=MESH),
        )

    def ways(q, way, act):
        to = me + 1 - 2 * way
        inside = me < line - 1 if way == 0 else me > 0
        to_end = to == line - 1 if way == 0 else to == 0
        to = lax.rem(to + line, line)

        @pl.when(inside)
        def _():
            for copy in copies(q, way, to)[:2]:
                act(copy)

        @pl.when(inside & jnp.logical_not(to_end))
        def _():
            act(copies(q, way, to)[2])

    def send(q, way):
        ways(q, way, lambda copy: copy.start())

    def arrive(q):
        parts = copies(q, 0, lax.rem(me + 1, line))
        parts[0].wait_recv()
        parts[1].wait_recv()

        @pl.when(jnp.logical_not(is_end))
        def _():
            parts[2].wait_recv()

    def end_copies():
        where = {"chol": mate}
        return (
            pltpu.make_async_remote_copy(half_hbm.at[:, :, cut:basis], half_end, end_send.at[0], end_recv.at[0],
                                         device_id=where, device_id_type=MESH),
            pltpu.make_async_remote_copy(slab_hbm.at[:, cut:basis, :], slab_end, end_send.at[1], end_recv.at[1],
                                         device_id=where, device_id_type=MESH),
        )

    def bias_copy(at):
        return pltpu.make_async_remote_copy(fbv.at[at], fbo.at[at], fb_send.at[at], fb_recv.at[at],
                                            device_id={"spin": 1 - spin}, device_id_type=MESH)

    def mate_copies(at, q):
        return [pltpu.make_async_remote_copy(
            fbv.at[at], fbe.at[i, q], mate_send.at[i, q], mate_recv.at[i, q],
            device_id={"chol": mate, "spin": spin + i * (1 - 2 * spin)}, device_id_type=MESH) for i in range(2)]

    def update_copy(q):
        return pltpu.make_async_remote_copy(upd.at[q], acc.at[me], upd_send.at[q], upd_recv.at[me],
                                            device_id={"chol": q}, device_id_type=MESH)

    def contribution(q, x, left, g):
        met = lax.dot_general(x, left, NT, preferred_element_type=jnp.float32)
        part = jnp.sum(met[:, 0:lanes] * invb[q, 0:tall, :].astype(jnp.float32), axis=0, keepdims=True)
        part = jnp.sum(part, axis=1, keepdims=True)
        packed = invb[q, tall:tall + 32, :].astype(jnp.float32)
        for i in range(tall // 32):
            beside = met[32 * i:32 * i + 32, lanes:elec] * packed[:, rest * i:rest * i + rest]
            part = part + jnp.sum(jnp.sum(beside, axis=0, keepdims=True), axis=1, keepdims=True)
        return -part

    def own_vectors(q, size):
        for g in range(vectors):
            field = root_three * (aux_ref[g, q * walks + wx].astype(jnp.float32) - 1.0)
            field = jnp.where(spin == 0, field, 0.0)
            fbv[q, g:g + 1, :] = jnp.broadcast_to(
                field + contribution(q, buf[q, :, 0:size], half[g, :, 0:size], g), (1, rows))
        bias_copy(q).start()

        @pl.when(is_end & (q != me))
        def _():
            for copy in mate_copies(q, q):
                copy.start()
        for g in range(vectors):
            item[q, g] = jnp.dot(buf[q, :, 0:size], slab[g, 0:size, :], preferred_element_type=jnp.float32)

    def compute(q):
        partial = is_end & (q != me)

        @pl.when(partial)
        def _():
            own_vectors(q, cut)

        @pl.when(jnp.logical_not(partial))
        def _():
            own_vectors(q, basis)

    def compute_end(q):
        for g in range(vectors):
            fbv[line + q, g:g + 1, :] = jnp.broadcast_to(
                contribution(q, buf[q, :, cut:basis], half_end[g], g), (1, rows))
        bias_copy(line + q).start()
        for copy in mate_copies(line + q, q):
            copy.start()
        for g in range(vectors):
            item[line + q, g] = jnp.dot(buf[q, :, cut:basis], slab_end[g], preferred_element_type=jnp.float32)

    def mates_sum(q):
        for copy in mate_copies(q, q):
            copy.wait_recv()
        return fbe[0, q] + fbe[1, q]

    def weighted(at, shift):
        value = None
        for g in range(vectors):
            term = item[at, g] * (shift[g:g + 1, :] * scale)
            value = term if value is None else value + term
        return value

    def updated(q):
        bias_copy(q).wait_recv()

        @pl.when(is_end & (q != me))
        def _():
            fbo[q] = fbo[q] + mates_sum(q)
        total[...] = weighted(q, fbv[q] + fbo[q])

        @pl.when(is_helper & (q != mate))
        def _():
            bias_copy(line + q).wait_recv()
            total[...] += weighted(line + q, fbv[line + q] + fbo[line + q] + mates_sum(q))

    def give(q):
        updated(q)
        upd[q] = total[...].astype(jnp.bfloat16)
        update_copy(q).start()

    send(me, 0)
    send(me, 1)

    @pl.when(is_end)
    def _():
        for copy in end_copies():
            copy.start()
    loads[2].wait()
    loads[3].wait()
    fbv[...] = jnp.zeros_like(fbv)

    def level(d, carry):
        above, below = me + d, me - d

        @pl.when((above < line) & (d > 0))
        def _():
            arrive(above)
            send(above, 1)

        @pl.when((below >= 0) & (d > 0))
        def _():
            arrive(below)
            send(below, 0)

        def meet(side, carry):
            q = me + d - 2 * d * side

            @pl.when((q >= 0) & (q < line) & ((d > 0) | (side == 0)))
            def _():
                compute(q)
            return carry

        def now(side, carry):
            q = me + d - 2 * d * side

            @pl.when((q >= 0) & (q < line) & (d > 0) & jnp.logical_not(is_end | (is_helper & (q != mate))))
            def _():
                give(q)
            return carry

        lax.fori_loop(0, 2, meet, 0)
        lax.fori_loop(0, 2, now, 0)
        return carry

    lax.fori_loop(0, line, level, 0)

    @pl.when(is_helper)
    def _():
        for copy in end_copies():
            copy.wait_recv()

    def help_end(t, carry):
        d, side = t // 2, t % 2
        q = me + d - 2 * d * side

        @pl.when((q >= 0) & (q < line) & ((d > 0) | (side == 0)) & is_helper & (q != mate))
        def _():
            compute_end(q)
        return carry

    def late(t, carry):
        d, side = t // 2, t % 2
        q = me + d - 2 * d * side

        @pl.when((q >= 0) & (q < line) & (d > 0) & (is_end | (is_helper & (q != mate))))
        def _():
            give(q)
        return carry

    lax.fori_loop(0, 2 * line, help_end, 0)
    lax.fori_loop(2, 2 * line, late, 0)

    updated(me)
    res[...] = orb[:, 0:rows] - total[0:elec, :]
    for k in range(1, line):
        q = lax.rem(me + k, line)
        pltpu.make_async_remote_copy(upd.at[q], acc.at[q], upd_send.at[q], upd_recv.at[q],
                                     device_id={"chol": q}, device_id_type=MESH).wait_recv()
        res[...] -= acc[q].astype(jnp.float32)[0:elec, :]
    leave = pltpu.make_async_copy(res, out_hbm.at[:, 0, :], load_sem.at[0])
    leave.start()

    def drain(q, carry):
        @pl.when(q <= me)
        def _():
            ways(q, 0, lambda copy: copy.wait_send())

        @pl.when(q >= me)
        def _():
            ways(q, 1, lambda copy: copy.wait_send())

        bias_copy(q).wait_send()

        @pl.when(is_helper & (q != mate))
        def _():
            bias_copy(line + q).wait_send()

        @pl.when((is_end | is_helper) & (q != end))
        def _():
            for copy in mate_copies(q, q):
                copy.wait_send()

        @pl.when(q != me)
        def _():
            update_copy(q).wait_send()
        return carry

    lax.fori_loop(0, line, drain, 0)

    @pl.when(is_end)
    def _():
        for copy in end_copies():
            copy.wait_send()
    leave.wait()


def body(orbitals, intersection_inv, half_chol, slab_chol, aux_field):
    line = lax.axis_size("chol")
    walks = lax.axis_size("walk")
    basis, elec = orbitals.shape[2:]
    vectors, rows = slab_chol.shape[:2]
    tall, wide = up_to(elec, 32), up_to(basis, 128)
    cut = wide - 256
    bf16, f32 = jnp.bfloat16, jnp.float32
    dma = pltpu.SemaphoreType.DMA
    any_spec = pl.BlockSpec(memory_space=pl.ANY)
    out = pl.pallas_call(
        functools.partial(kernel, line, walks),
        out_shape=jax.ShapeDtypeStruct((elec, 1, rows), f32),
        in_specs=[any_spec] * 4 + [pl.BlockSpec(memory_space=pltpu.SMEM)],
        out_specs=any_spec,
        scratch_shapes=[
            pltpu.VMEM((elec, basis), f32),
            pltpu.VMEM((elec, elec), f32),
            pltpu.VMEM((vectors, elec, basis), bf16),
            pltpu.VMEM((vectors, basis, rows), bf16),
            pltpu.VMEM((vectors, elec, basis - cut), bf16),
            pltpu.VMEM((vectors, basis - cut, rows), bf16),
            pltpu.VMEM((elec, rows), f32),
            pltpu.VMEM((line, tall, wide), bf16),
            pltpu.VMEM((line, tall + 32, 128), bf16),
            pltpu.VMEM((2 * line, vectors, tall, rows), f32),
            pltpu.VMEM((2 * line, up_to(vectors, 8), rows), f32),
            pltpu.VMEM((2 * line, up_to(vectors, 8), rows), f32),
            pltpu.VMEM((2, line, up_to(vectors, 8), rows), f32),
            pltpu.VMEM((line, tall, rows), bf16),
            pltpu.VMEM((line, tall, rows), bf16),
            pltpu.VMEM((tall, rows), f32),
            dma((4,)),
            dma((2, 2, line)), dma((2, line)),
            dma((2, line)), dma((line,)),
            dma((2 * line,)), dma((2 * line,)),
            dma((2, line)), dma((2, line)),
            dma((line,)), dma((line,)),
            dma((2,)), dma((2,)),
        ],
        compiler_params=pltpu.CompilerParams(
            collective_id=0, has_side_effects=True, vmem_limit_bytes=63 * 1024 * 1024
        ),
    )(
        jnp.transpose(orbitals[0], (2, 0, 1)), jnp.transpose(intersection_inv[0], (1, 0, 2)),
        half_chol[:, 0], jnp.transpose(slab_chol, (0, 2, 1)), jnp.transpose(aux_field),
    )
    return jnp.transpose(out, (1, 2, 0))[None]


def solution(mesh):
    placed = (
        P(("groups", "chol", "walk"), "spin", None, None),
        P(("groups", "chol", "walk"), "spin", None, None),
        P("chol", "spin", None, None),
        P("chol", None, None),
        P("groups", "chol"),
    )
    return jax.shard_map(
        body,
        mesh=mesh,
        in_specs=placed,
        out_specs=P(("groups", "chol", "walk"), "spin", None, None),
        check_vma=False,
    )
```

time: 53.2 us -> 52.1 us (0.979)
  Pallas kernels: 51.4 us -> 50.2 us
    pallas_call x1, Pallas kernels: 51.4 us -> 50.2 us  [body(): pl.pallas_call(functools.partial(kernel, line, walks), out_shape=jax.Shap...]
where the time goes in v3:
time: 52.1 us; the launch traced here: 51.9 us
  Pallas kernels  50.2 us (96%)
  local copies, waits for them, and re-layouts  1.68 us (3%)
    pallas_call x1, Pallas kernels, body(): pl.pallas_call(functools.partial(kernel, line, walks), out_shape=jax.Shap...  50.2 us
    unnamed x1, local copies, waits for them, and re-layouts  1.68 us

profile of v3, /device:TPU:0, one launch (start us, length us, event | category | flops | bytes accessed | tf_op | source)
XLA Modules:
  0.0 51.9 jit_solution(16556104508195248993)
XLA Ops:
  0.0 50.2 %shard_map.55 = f32[150,1,256]{2,1,0:T(1,128)} custom-call(f32[150,1,1400]{2,1,0:T(1,128)} %bitcast.14, f32[150,1,150]{2,1,0:T(1,128)} %bitcast.16, bf16[3,150,1400]{2,1,0:T(8,128)(2,1)} %bitcast.13, bf16[3,1400,256]{2,1,0:T(8,128)(2,1)} %bitcast.12, s32[3,8]{1,0:T(4,128)} %bitcast.17), custom_call_target="tpu_custom_call" | custom-call | tf_op jit(solution)/shard_map/pallas_call | solution.py:337
  50.2 1.7 %copy.8 = f32[1,1,256,150]{2,1,3,0:T(1,128)} copy(f32[1,1,256,150]{2,1,3,0:T(1,128)} %bitcast.15) | data formatting | bytes 307200

commit v4 on v3

--- a/solution.py
+++ b/solution.py
@@ -19,7 +19,7 @@
 
 def kernel(line, walks, orb_hbm, inv_hbm, half_hbm, slab_hbm, aux_ref, out_hbm,
            orb, inv, half, slab, half_end, slab_end, res, buf, invb, item, fbv, fbo, fbe, upd, acc, total, load_sem,
-           walk_send, walk_recv, inv_send, inv_recv, fb_send, fb_recv, mate_send, mate_recv, upd_send, upd_recv,
+           walk_send, walk_recv, fb_send, fb_recv, mate_send, mate_recv, upd_send, upd_recv,
            end_send, end_recv):
     me = lax.axis_index("chol")
     spin = lax.axis_index("spin")
@@ -52,10 +52,10 @@
     def _():
         pl.semaphore_signal(barrier, inc=1, device_id={"chol": mate, "spin": 1 - spin}, device_id_type=MESH)
 
-    loads[0].wait()
-    loads[1].wait()
+    bounds = [0, 384, 768, cut, wide]
     eye = (lax.broadcasted_iota(jnp.int32, (tall, elec), 0)
            == lax.broadcasted_iota(jnp.int32, (tall, elec), 1)).astype(jnp.bfloat16)
+    loads[1].wait()
     tall_inv = jnp.dot(eye, inv[...].astype(jnp.bfloat16), preferred_element_type=jnp.float32)
     invb[me, 0:tall, :] = tall_inv[:, 0:lanes].astype(jnp.bfloat16)
     side = [tall_inv[at:at + 32, lanes:elec] for at in range(0, tall, 32)]
@@ -64,51 +64,32 @@
     full = elec // 16 * 16
     last = basis // 128 * 128
     buf[me, :, last:wide] = jnp.zeros((tall, wide - last), jnp.bfloat16)
-    buf[me, 0:full, 0:basis] = orb[0:full, :].astype(jnp.bfloat16)
-    buf[me, full:tall, 0:basis] = jnp.dot(
-        eye[0:tall - full, 0:elec - full], orb[full:elec, :].astype(jnp.bfloat16),
-        preferred_element_type=jnp.float32).astype(jnp.bfloat16)
-
+    loads[0].wait()
     pl.semaphore_wait(barrier, line + jnp.where(is_end | is_helper, 1, 0))
 
-    def copies(q, way, to):
-        where = {"chol": to}
-        first, last = buf.at[q, :, 0:cut], buf.at[q, :, cut:wide]
-        return (
-            pltpu.make_async_remote_copy(invb.at[q], invb.at[q], inv_send.at[way, q], inv_recv.at[q],
-                                         device_id=where, device_id_type=MESH),
-            pltpu.make_async_remote_copy(first, first, walk_send.at[way, 0, q], walk_recv.at[0, q],
-                                         device_id=where, device_id_type=MESH),
-            pltpu.make_async_remote_copy(last, last, walk_send.at[way, 1, q], walk_recv.at[1, q],
-                                         device_id=where, device_id_type=MESH),
-        )
-
-    def ways(q, way, act):
+    def piece(q, way, c, to):
+        ref = invb.at[q] if c == 0 else buf.at[q, :, bounds[c - 1]:bounds[c]]
+        return pltpu.make_async_remote_copy(ref, ref, walk_send.at[way, c, q], walk_recv.at[c, q],
+                                            device_id={"chol": to}, device_id_type=MESH)
+
+    def move(q, way, c, act):
         to = me + 1 - 2 * way
         inside = me < line - 1 if way == 0 else me > 0
         to_end = to == line - 1 if way == 0 else to == 0
-        to = lax.rem(to + line, line)
+        if c == len(bounds) - 1:
+            inside = inside & jnp.logical_not(to_end)
 
         @pl.when(inside)
         def _():
-            for copy in copies(q, way, to)[:2]:
-                act(copy)
-
-        @pl.when(inside & jnp.logical_not(to_end))
-        def _():
-            act(copies(q, way, to)[2])
-
-    def send(q, way):
-        ways(q, way, lambda copy: copy.start())
-
-    def arrive(q):
-        parts = copies(q, 0, lax.rem(me + 1, line))
-        parts[0].wait_recv()
-        parts[1].wait_recv()
-
-        @pl.when(jnp.logical_not(is_end))
-        def _():
-            parts[2].wait_recv()
+            act(piece(q, way, c, lax.rem(to + line, line)))
+
+    def arrive(q, way, c):
+        wanted = jnp.logical_not(is_end) if c == len(bounds) - 1 else me >= 0
+
+        @pl.when(wanted)
+        def _():
+            piece(q, 0, c, lax.rem(me + 1, line)).wait_recv()
+            move(q, way, c, lambda copy: copy.start())
 
     def end_copies():
         where = {"chol": mate}
@@ -208,8 +189,15 @@
         upd[q] = total[...].astype(jnp.bfloat16)
         update_copy(q).start()
 
-    send(me, 0)
-    send(me, 1)
+    for c in range(len(bounds)):
+        if c > 0:
+            low, high = bounds[c - 1], min(bounds[c], basis)
+            buf[me, 0:full, low:high] = orb[0:full, low:high].astype(jnp.bfloat16)
+            buf[me, full:tall, low:high] = jnp.dot(
+                eye[0:tall - full, 0:elec - full], orb[full:elec, low:high].astype(jnp.bfloat16),
+                preferred_element_type=jnp.float32).astype(jnp.bfloat16)
+        for way in range(2):
+            move(me, way, c, lambda copy: copy.start())
 
     @pl.when(is_end)
     def _():
@@ -222,15 +210,14 @@
     def level(d, carry):
         above, below = me + d, me - d
 
-        @pl.when((above < line) & (d > 0))
-        def _():
-            arrive(above)
-            send(above, 1)
-
-        @pl.when((below >= 0) & (d > 0))
-        def _():
-            arrive(below)
-            send(below, 0)
+        for c in range(len(bounds)):
+            @pl.when((above < line) & (d > 0))
+            def _():
+                arrive(above, 1, c)
+
+            @pl.when((below >= 0) & (d > 0))
+            def _():
+                arrive(below, 0, c)
 
         def meet(side, carry):
             q = me + d - 2 * d * side
@@ -269,7 +256,7 @@
         return carry
 
     def late(t, carry):
-        d, side = t // 2, t % 2
+        d, side = line - 1 - t // 2, t % 2
         q = me + d - 2 * d * side
 
         @pl.when((q >= 0) & (q < line) & (d > 0) & (is_end | (is_helper & (q != mate))))
@@ -278,7 +265,7 @@
         return carry
 
     lax.fori_loop(0, 2 * line, help_end, 0)
-    lax.fori_loop(2, 2 * line, late, 0)
+    lax.fori_loop(0, 2 * line - 2, late, 0)
 
     updated(me)
     res[...] = orb[:, 0:rows] - total[0:elec, :]
@@ -293,11 +280,13 @@
     def drain(q, carry):
         @pl.when(q <= me)
         def _():
-            ways(q, 0, lambda copy: copy.wait_send())
+            for c in range(len(bounds)):
+                move(q, 0, c, lambda copy: copy.wait_send())
 
         @pl.when(q >= me)
         def _():
-            ways(q, 1, lambda copy: copy.wait_send())
+            for c in range(len(bounds)):
+                move(q, 1, c, lambda copy: copy.wait_send())
 
         bias_copy(q).wait_send()
 
@@ -357,8 +346,7 @@
             pltpu.VMEM((line, tall, rows), bf16),
             pltpu.VMEM((tall, rows), f32),
             dma((4,)),
-            dma((2, 2, line)), dma((2, line)),
-            dma((2, line)), dma((line,)),
+            dma((2, 5, line)), dma((5, line)),
             dma((2 * line,)), dma((2 * line,)),
             dma((2, line)), dma((2, line)),
             dma((line,)), dma((line,)),

time: 52.1 us -> 49.5 us (0.950)
  Pallas kernels: 50.2 us -> 47.6 us
    pallas_call x1, Pallas kernels: 50.2 us -> 47.6 us  [body(): pl.pallas_call(functools.partial(kernel, line, walks), out_shape=jax.Shap...]
where the time goes in v4:
time: 49.5 us; the launch traced here: 49.3 us
  Pallas kernels  47.6 us (96%)
  local copies, waits for them, and re-layouts  1.68 us (3%)
    pallas_call x1, Pallas kernels, body(): pl.pallas_call(functools.partial(kernel, line, walks), out_shape=jax.Shap...  47.6 us
    unnamed x1, local copies, waits for them, and re-layouts  1.68 us

profile of v4, /device:TPU:0, one launch (start us, length us, event | category | flops | bytes accessed | tf_op | source)
XLA Modules:
  0.0 49.3 jit_solution(1691468872867812469)
XLA Ops:
  0.0 47.6 %shard_map.55 = f32[150,1,256]{2,1,0:T(1,128)} custom-call(f32[150,1,1400]{2,1,0:T(1,128)} %bitcast.14, f32[150,1,150]{2,1,0:T(1,128)} %bitcast.16, bf16[3,150,1400]{2,1,0:T(8,128)(2,1)} %bitcast.13, bf16[3,1400,256]{2,1,0:T(8,128)(2,1)} %bitcast.12, s32[3,8]{1,0:T(4,128)} %bitcast.17), custom_call_target="tpu_custom_call" | custom-call | tf_op jit(solution)/shard_map/pallas_call | solution.py:326
  47.7 1.7 %copy.8 = f32[1,1,256,150]{2,1,3,0:T(1,128)} copy(f32[1,1,256,150]{2,1,3,0:T(1,128)} %bitcast.15) | data formatting | bytes 307200

commit v5 on v4

--- a/solution.py
+++ b/solution.py
@@ -91,14 +91,21 @@
             piece(q, 0, c, lax.rem(me + 1, line)).wait_recv()
             move(q, way, c, lambda copy: copy.start())
 
+    share = pl.ds(pl.multiple_of(spin * (rows // 2), rows // 2), rows // 2)
+
     def end_copies():
         where = {"chol": mate}
         return (
             pltpu.make_async_remote_copy(half_hbm.at[:, :, cut:basis], half_end, end_send.at[0], end_recv.at[0],
                                          device_id=where, device_id_type=MESH),
-            pltpu.make_async_remote_copy(slab_hbm.at[:, cut:basis, :], slab_end, end_send.at[1], end_recv.at[1],
-                                         device_id=where, device_id_type=MESH),
+            pltpu.make_async_remote_copy(slab_hbm.at[:, cut:basis, share], slab_end.at[:, :, share],
+                                         end_send.at[1], end_recv.at[1], device_id=where, device_id_type=MESH),
         )
+
+    def share_copy():
+        return pltpu.make_async_remote_copy(slab_end.at[:, :, share], slab_end.at[:, :, share],
+                                            end_send.at[2], end_recv.at[2],
+                                            device_id={"spin": 1 - spin}, device_id_type=MESH)
 
     def bias_copy(at):
         return pltpu.make_async_remote_copy(fbv.at[at], fbo.at[at], fb_send.at[at], fb_recv.at[at],
@@ -243,8 +250,11 @@
 
     @pl.when(is_helper)
     def _():
-        for copy in end_copies():
-            copy.wait_recv()
+        first, second = end_copies()
+        second.wait_recv()
+        share_copy().start()
+        first.wait_recv()
+        share_copy().wait_recv()
 
     def help_end(t, carry):
         d, side = t // 2, t % 2
@@ -310,6 +320,10 @@
     def _():
         for copy in end_copies():
             copy.wait_send()
+
+    @pl.when(is_helper)
+    def _():
+        share_copy().wait_send()
     leave.wait()
 
 
@@ -319,7 +333,7 @@
     basis, elec = orbitals.shape[2:]
     vectors, rows = slab_chol.shape[:2]
     tall, wide = up_to(elec, 32), up_to(basis, 128)
-    cut = wide - 256
+    cut = wide - 384
     bf16, f32 = jnp.bfloat16, jnp.float32
     dma = pltpu.SemaphoreType.DMA
     any_spec = pl.BlockSpec(memory_space=pl.ANY)
@@ -350,7 +364,7 @@
             dma((2 * line,)), dma((2 * line,)),
             dma((2, line)), dma((2, line)),
             dma((line,)), dma((line,)),
-            dma((2,)), dma((2,)),
+            dma((3,)), dma((3,)),
         ],
         compiler_params=pltpu.CompilerParams(
             collective_id=0, has_side_effects=True, vmem_limit_bytes=63 * 1024 * 1024

time: 49.5 us -> 47.9 us (0.968)
  Pallas kernels: 47.6 us -> 46.1 us
    pallas_call x1, Pallas kernels: 47.6 us -> 46.1 us  [body(): pl.pallas_call(functools.partial(kernel, line, walks), out_shape=jax.Shap...]
where the time goes in v5:
time: 47.9 us; the launch traced here: 47.8 us
  Pallas kernels  46.1 us (96%)
  local copies, waits for them, and re-layouts  1.68 us (4%)
    pallas_call x1, Pallas kernels, body(): pl.pallas_call(functools.partial(kernel, line, walks), out_shape=jax.Shap...  46.1 us
    unnamed x1, local copies, waits for them, and re-layouts  1.68 us

profile of v5, /device:TPU:0, one launch (start us, length us, event | category | flops | bytes accessed | tf_op | source)
XLA Modules:
  0.0 47.8 jit_solution(14033233204263736934)
XLA Ops:
  0.0 46.1 %shard_map.55 = f32[150,1,256]{2,1,0:T(1,128)} custom-call(f32[150,1,1400]{2,1,0:T(1,128)} %bitcast.14, f32[150,1,150]{2,1,0:T(1,128)} %bitcast.16, bf16[3,150,1400]{2,1,0:T(8,128)(2,1)} %bitcast.13, bf16[3,1400,256]{2,1,0:T(8,128)(2,1)} %bitcast.12, s32[3,8]{1,0:T(4,128)} %bitcast.17), custom_call_target="tpu_custom_call" | custom-call | tf_op jit(solution)/shard_map/pallas_call | solution.py:340
  46.1 1.7 %copy.8 = f32[1,1,256,150]{2,1,3,0:T(1,128)} copy(f32[1,1,256,150]{2,1,3,0:T(1,128)} %bitcast.15) | data formatting | bytes 307200
